TPU v7x, 32 devices: a whole 2x2x4 slice. The times are simulated.
32 devices in a mesh: grp: 2 (over y), pos: 16 (over z, x, core).
Axes of the slice: x: 2, y: 2, z: 4, core: 2. Of those that a mesh axis runs over, the one named last changes fastest.
Arguments:
- sequences: int32 [1024, 128], P(('grp', 'pos')), parts along dimension 0, may hold values from 0 to 20
- fields: float32 [1024, 21], P(('grp', 'pos')), parts along dimension 0, may hold values from -3 to 3
- band_coupling: float32 [1024, 16, 441], P(('grp', 'pos')), parts along dimension 0, may hold values from -1 to 1
- contact_coupling: float32 [32, 16, 8, 441], P(('grp', 'pos')), parts along dimension 0, may hold values from -1.6 to 1.6
- slot_start: int32 [32, 16, 8], P(('grp', 'pos')), parts along dimension 0, may hold values from -1 to 31, as said below
- slot_end: int32 [32, 16, 8], P(('grp', 'pos')), parts along dimension 0, may hold values from -1 to 31, as said below
- seq_weight: float32 [256], P('grp'), parts along dimension 0, may hold values from 0.02 to 0.25
Outputs:
- grad_band: float32 [1024, 16, 441], P(('grp', 'pos')), parts along dimension 0
- grad_contact: float32 [32, 16, 8, 441], P(('grp', 'pos')), parts along dimension 0
- grad_field: float32 [1024, 21], P(('grp', 'pos')), parts along dimension 0
There are 2 independent parts, one for each index of `grp`. A program takes and returns all parts, laid end to end along the dimension named above; each array names one. Nothing has to cross between parts.
Inputs may be any that keep to these rules, and one draw needn't show every extreme that they name: `slot_start`: entry [d, e, c] is the position, within the block of 32 positions of device d, where contact slot c from device d to device e begins, or -1 where that slot is empty. `slot_end`: entry [e, d, c] is the position, within the block of device e, where the contact of slot c from device d to device e ends; it is -1 exactly where slot_start[d, e, c] is -1, and a contact never joins a position to itself.
All inputs are finite; a program needn't handle non-finite values.
Results may differ from a plain program's by a relative error of at most 0.0001.
Values sent between devices are 32-bit elements; how exact they have to be, the bound alone decides.
A program may use at most 128 MiB of HBM per device.

v0:
```python
import jax
import jax.numpy as jnp
from jax import lax
from jax.sharding import PartitionSpec as P

precise = lax.Precision.HIGHEST


def shifted(value, axis, by):
    size = lax.axis_size(axis)
    pairs = [(i, i + by) for i in range(size) if 0 <= i + by < size]
    return lax.ppermute(value, axis, pairs)


def with_halo(block, sides, width):
    for axis, dim in sides:
        count = lax.axis_size(axis)
        forward = [(i, i + 1) for i in range(count - 1)]
        backward = [(target, source) for source, target in forward]
        low = lax.ppermute(
            lax.slice_in_dim(block, block.shape[dim] - width, None, axis=dim), axis, forward
        )
        high = lax.ppermute(lax.slice_in_dim(block, 0, width, axis=dim), axis, backward)
        block = jnp.concatenate([low, block, high], axis=dim)
    return block


def hot_states(sequences, states):
    levels = jnp.arange(states, dtype=jnp.int32)
    return (sequences[:, None, :] == levels[None, :, None]).astype(jnp.float32)


def lift_rows(blocks, one_hot):
    return jnp.einsum("sab,san->sbn", blocks, one_hot, precision=precise)


def pull_columns(blocks, one_hot):
    return jnp.einsum("sab,sbn->san", blocks, one_hot, precision=precise)


def pair_terms(left_res, left_hot, right_hot, right_res):
    first = jnp.einsum("san,sbn->sab", left_res, right_hot, precision=precise)
    return first + jnp.einsum("san,sbn->sab", left_hot, right_res, precision=precise)


def from_next(payload):
    return shifted(payload, "pos", -1)


def rim_pull(blocks, front_hot, band_width, blank_rows):
    offsets = jnp.arange(band_width, dtype=jnp.int32)
    back_pull = blank_rows
    for offset in range(1, band_width + 1):
        in_reach = (offsets + offset >= band_width).astype(jnp.float32)[:, None, None]
        pulled = pull_columns(blocks[:, offset - 1], front_hot[offset : offset + band_width])
        back_pull = back_pull + in_reach * pulled
    return back_pull


def on_device(sequences, fields, band_coupling, contact_coupling, slot_start, slot_end, seq_weight):
    rows_here, seq_count = sequences.shape
    states = fields.shape[1]
    band_width = band_coupling.shape[1]
    devices = contact_coupling.shape[1]
    slot_depth = contact_coupling.shape[2]
    total_slots = devices * slot_depth
    band_blocks = band_coupling.reshape(rows_here, band_width, states, states)
    one_hot = hot_states(sequences, states)
    blank_rows = jnp.zeros((band_width, states, seq_count), jnp.float32)
    logits = jnp.broadcast_to(fields[:, :, None], one_hot.shape)
    spill_over = blank_rows
    for offset in range(1, band_width + 1):
        kept_rows = rows_here - offset
        blocks_now = band_blocks[:, offset - 1]
        lifted = lift_rows(blocks_now, one_hot)
        logits = logits.at[offset:].add(lifted[:kept_rows])
        spill_over = spill_over.at[:offset].add(lifted[kept_rows:])
        pulled = pull_columns(blocks_now[:kept_rows], one_hot[offset:])
        logits = logits.at[:kept_rows].add(pulled)
    rim_blocks = band_blocks[rows_here - band_width :]
    front_hot = jnp.concatenate([blank_rows, one_hot[:band_width]], 0)
    prev_blocks, prev_spill = shifted((rim_blocks, spill_over), "pos", 1)
    logits = logits.at[:band_width].add(prev_spill)
    back_pull = rim_pull(prev_blocks, front_hot, band_width, blank_rows)
    logits = logits.at[rows_here - band_width :].add(from_next(back_pull))
    slot_blocks = contact_coupling[0].reshape(total_slots, states, states)
    starts = slot_start[0].reshape(total_slots)
    live_slots = (starts >= 0).astype(jnp.float32)
    start_safe = jnp.maximum(starts, 0)
    slot_blocks = slot_blocks * live_slots[:, None, None]
    start_ids = sequences[start_safe]
    end_rows = slot_end[0].reshape(total_slots)
    end_live = (end_rows >= 0).astype(jnp.float32)
    end_safe = jnp.maximum(end_rows, 0)
    end_ids = sequences[end_safe]
    end_hot = one_hot[end_safe]
    positions = jnp.arange(rows_here, dtype=jnp.int32)
    start_pick = (positions[:, None] == start_safe[None, :]).astype(jnp.float32) * live_slots[
        None, :
    ]
    end_pick = (positions[:, None] == end_safe[None, :]).astype(jnp.float32) * end_live[None, :]
    slot_shape = (devices, slot_depth, states, seq_count)
    flat_shape = (total_slots, states, seq_count)
    arrived_blocks, remote_ids, returned_ids = (
        lax.all_to_all(
            slot_blocks.reshape(devices, slot_depth, states * states),
            "pos",
            split_axis=0,
            concat_axis=0,
            tiled=True,
        ),
        lax.all_to_all(
            start_ids.reshape(devices, slot_depth, seq_count),
            "pos",
            split_axis=0,
            concat_axis=0,
            tiled=True,
        ),
        lax.all_to_all(
            end_ids.reshape(devices, slot_depth, seq_count),
            "pos",
            split_axis=0,
            concat_axis=0,
            tiled=True,
        ),
    )
    arrived_blocks = arrived_blocks.reshape(total_slots, states, states)
    remote_ids = remote_ids.reshape(total_slots, seq_count)
    remote_hot = hot_states(remote_ids, states)
    arrived_rows = lift_rows(arrived_blocks, remote_hot)
    returned_ids = returned_ids.reshape(total_slots, seq_count)
    came_back = pull_columns(slot_blocks, hot_states(returned_ids, states))
    logits = logits + jnp.einsum("ps,sqn->pqn", end_pick, arrived_rows, precision=precise)
    logits = logits + jnp.einsum("ps,sqn->pqn", start_pick, came_back, precision=precise)
    exp_logits = jnp.exp(logits)
    probability = exp_logits / jnp.sum(exp_logits, axis=1, keepdims=True)
    residual = seq_weight[None, None, :] * (probability - one_hot)
    grad_field = jnp.sum(residual, axis=2)
    padded = with_halo(residual, (("pos", 0),), band_width)
    prev_res = padded[:band_width]
    ahead_res = jnp.concatenate([residual, padded[rows_here + band_width :]], 0)
    ghost_hot = jnp.concatenate([one_hot, blank_rows], 0)
    grads = []
    rim_terms = []
    for offset in range(1, band_width + 1):
        grads.append(
            pair_terms(
                residual,
                one_hot,
                ghost_hot[offset : offset + rows_here],
                ahead_res[offset : offset + rows_here],
            )
        )
        rim_terms.append(
            jnp.einsum(
                "ran,rbn->rab", prev_res, front_hot[offset : offset + band_width], precision=precise
            )
        )
    grad_band = jnp.stack(grads, 1)
    back_terms = from_next(jnp.stack(rim_terms, 1))
    grad_band = grad_band.at[rows_here - band_width :].add(back_terms)
    start_res = residual[start_safe]
    end_res = residual[end_safe]
    arrived_res = lax.all_to_all(
        start_res.reshape(slot_shape), "pos", split_axis=0, concat_axis=0, tiled=True
    ).reshape(flat_shape)
    near_terms = pair_terms(arrived_res, remote_hot, end_hot, end_res) * end_live[:, None, None]
    returned_terms = lax.all_to_all(
        near_terms.reshape(devices, slot_depth, states * states),
        "pos",
        split_axis=0,
        concat_axis=0,
        tiled=True,
    ).reshape(total_slots, states, states)
    grad_contact = returned_terms * live_slots[:, None, None]
    return (
        grad_band.reshape(rows_here, band_width, states * states),
        grad_contact.reshape(1, devices, slot_depth, states * states),
        grad_field,
    )


def solution(mesh):
    in_specs = (
        P(("grp", "pos"), None),
        P(("grp", "pos"), None),
        P(("grp", "pos"), None, None),
        P(("grp", "pos"), None, None, None),
        P(("grp", "pos"), None, None),
        P(("grp", "pos"), None, None),
        P("grp"),
    )
    out_specs = (
        P(("grp", "pos"), None, None),
        P(("grp", "pos"), None, None, None),
        P(("grp", "pos"), None),
    )
    return jax.shard_map(
        on_device, mesh=mesh, in_specs=in_specs, out_specs=out_specs, check_vma=False
    )
```

profile of v0, /device:TPU:11, one launch (start us, length us, event | category | flops | bytes accessed | tf_op | source)
XLA Modules:
  0.0 314.5 jit_solution(17761578838836654088)
XLA Ops:
  2.1 2.0 gather_fusion.1
  4.1 6.6 %all-to-all-start.2 = ((s32[16,8,128]{2,1,0:T(8,128)}), s32[16,8,128]{2,1,0:T(8,128)}, u32[]{:S(2)}, u32[]{:S(2)}) async-start(s32[16,8,128]{2,1,0:T(8,128)} %bitcast.88), calls=%async_computation.2 | async-start | bytes 131072 | tf_op jit(solution)/shard_map/all_to_all | solution.py:119
  12.2 3.7 %copy.84 = f32[32,16,441]{0,1,2:T(8,128)} copy(f32[32,16,441]{2,1,0:T(8,128)} %param.113) | data formatting | bytes 1806336 | tf_op args[2]
  15.9 14.8 %fusion.348 = (f32[32,1,21,21]{0,1,3,2:T(1,128)S(1)}, f32[32,1,21,21]{0,1,3,2:T(1,128)S(1)}, f32[32,1,21,21]{0,1,3,2:T(1,128)}, f32[32,1,21,21]{0,1,3,2:T(1,128)...) fusion(f32[32,16,21,21]{0,1,3,2:T(8,128)} %bitcast.458), kind=kLoop, calls=%fused_computation.564 | loop fusion | bytes 1806336 | tf_op jit(solution)/shard_map/slice | solution.py:74
  67.7 2.3 convolution_bitcast_fusion
  70.1 2.0 copy.153
  73.4 1.6 fusion.54
  76.9 1.5 fusion.58
  80.4 1.6 fusion.50
  104.9 3.5 %collective-permute-start = (f32[16,21,128]{2,1,0:T(8,128)}, f32[16,21,128]{2,1,0:T(8,128)}, u32[]{:S(2)}, u32[]{:S(2)}) collective-permute-start(f32[16,21,128]{2,1,0:T(8,128)} %get-tuple-element.668), channel_id=1, source_target_pairs={{0,1},{1,2},{2,3},{3,4},{4,5},{5,6},{6,7},{7,8},{8,9},{9,10},{10,1... | collective-permute-start | bytes 516104 | tf_op jit(solution)/shard_map/ppermute | solution.py:12
  109.3 2.0 slice.1890
  111.4 2.0 copy.117
  113.4 2.2 collective-permute-start.1
  115.7 1.7 slice.2045
  120.7 1.7 bitcast_multiply_fusion
  126.5 6.1 %all-to-all-start = ((f32[16,8,441]{2,1,0:T(8,128)}), f32[16,8,441]{2,1,0:T(8,128)}, u32[]{:S(2)}, u32[]{:S(2)}) async-start(f32[16,8,441]{2,1,0:T(8,128)} %bitcast_multiply_fusion), calls=%async_computation | async-start | bytes 524288 | tf_op jit(solution)/shard_map/all_to_all | solution.py:105
  132.5 2.5 fusion.1
  136.0 15.5 %all-to-all-done = f32[16,8,441]{2,1,0:T(8,128)} async-done(((f32[16,8,441]{2,1,0:T(8,128)}), f32[16,8,441]{2,1,0:T(8,128)}, u32[]{:S(2)}, u32[]{:S(2)}) %all-to-all-start) | async-done | bytes 225824 | tf_op jit(solution)/shard_map/all_to_all | solution.py:105
  151.6 7.5 %all-to-all-start.1 = ((s32[16,8,128]{2,1,0:T(8,128)}), s32[16,8,128]{2,1,0:T(8,128)S(1)}, u32[]{:S(2)}, u32[]{:S(2)}) async-start(s32[16,8,128]{2,1,0:T(8,128)} %bitcast.480), calls=%async_computation.1 | async-start | bytes 131072 | tf_op jit(solution)/shard_map/all_to_all | solution.py:112
  161.6 1.6 all-to-all-done.1
  163.2 1.6 fusion.4
  164.8 10.3 %fusion.349 = (f32[16,1,21,21]{3,1,2,0:T(1,128)S(1)}, f32[16,1,21,21]{3,1,2,0:T(1,128)S(1)}, f32[16,1,21,21]{3,1,2,0:T(1,128)S(1)}, f32[16,1,21,21]{3,1,2,0:T(1,...) fusion(f32[16,16,21,21]{3,1,2,0:T(8,128)} %collective-permute-d, ...), kind=kLoop, calls=%fused_computation.565 | loop fusion | bytes 903168 | tf_op jit(solution)/shard_map/slice | solution.py:55
  182.5 2.5 collective-permute-start.2
  185.9 4.4 %collective-permute-done.2 = f32[16,21,128]{2,1,0:T(8,128)S(1)} collective-permute-done((f32[16,21,128]{2,1,0:T(8,128)S(1)}, f32[16,21,128]{2,1,0:T(8,128)S(1)}, u32[]{:S(2)}, u32[]{:S(2)}) %collective-permute-start.2) | collective-permute-done | bytes 172064 | tf_op jit(solution)/shard_map/ppermute | solution.py:12
  191.4 1.5 fusion.138
  195.1 1.5 fusion.140
  198.1 1.5 fusion.142
  204.1 1.5 fusion.146
  205.7 1.5 fusion.147
  207.2 1.5 fusion.148
  210.2 1.5 fusion.150
  211.7 1.9 fusion.151
  213.6 1.5 fusion.152
  215.1 2.0 gather_fusion.2
  218.0 1.9 collective-permute-start.3
  219.9 4.5 %collective-permute-start.4 = (f32[16,21,128]{2,1,0:T(8,128)}, f32[16,21,128]{2,1,0:T(8,128)S(1)}, u32[]{:S(2)}, u32[]{:S(2)}) collective-permute-start(f32[16,21,128]{2,1,0:T(8,128)} %get-tuple-element.666), channel_id=1, source_target_pairs={{0,1},{1,2},{2,3},{3,4},{4,5},{5,6},{6,7},{7,8},{8,9},{9,10},{10,1... | collective-permute-start | bytes 516104 | tf_op jit(solution)/shard_map/ppermute | solution.py:20
  224.5 2.8 copy.147
  227.2 4.3 %all-to-all-start.3 = ((f32[16,8,21,128]{3,1,2,0:T(8,128)}), f32[16,8,21,128]{3,1,2,0:T(8,128)}, u32[]{:S(2)}, u32[]{:S(2)}) async-start(f32[16,8,21,128]{3,1,2,0:T(8,128)} %copy.147), calls=%async_computation.3 | async-start | bytes 2752512 | tf_op jit(solution)/shard_map/all_to_all | solution.py:164
  240.1 3.1 copy.144
  243.3 2.3 collective-permute-start.5
  265.4 1.6 copy.148
  268.4 2.7 add_multiply_fusion
  271.1 2.5 reshape.1685
  273.6 7.4 %all-to-all-start.4 = ((f32[16,8,441]{2,1,0:T(8,128)}), f32[16,8,441]{2,1,0:T(8,128)S(1)}, u32[]{:S(2)}, u32[]{:S(2)}) async-start(f32[16,8,441]{2,1,0:T(8,128)} %reshape.1685), calls=%async_computation.4 | async-start | bytes 524288 | tf_op jit(solution)/shard_map/all_to_all | solution.py:168
  281.0 16.0 %collective-permute-done.5 = f32[16,16,21,21]{3,1,2,0:T(8,128)} collective-permute-done((f32[16,16,21,21]{3,1,2,0:T(8,128)}, f32[16,16,21,21]{3,1,2,0:T(8,128)}, u32[]{:S(2)}, u32[]{:S(2)}) %collective-permute-start.5) | collective-permute-done | bytes 451616 | tf_op jit(solution)/shard_map/ppermute | solution.py:12
  297.0 5.4 %fusion = f32[32,16,21,21]{3,2,0,1:T(8,128)} fusion(f32[32,16,21,21]{3,2,0,1:T(8,128)} %fusion.10, f32[16,16,21,21]{3,1,2,0:T(8,128)} %collective-permute-done.5), kind=kLoop, calls=%fused_computation.6 | loop fusion | flops 112896 | bytes 9043968 | tf_op jit(solution)/shard_map/scatter-add | solution.py:161
  302.4 7.3 %copy.146 = f32[32,16,21,21]{0,1,3,2:T(8,128)} copy(f32[32,16,21,21]{3,2,0,1:T(8,128)} %fusion) | data formatting | bytes 1806336 | tf_op jit(solution)/shard_map/scatter-add | solution.py:161
  309.7 3.8 %copy.149 = f32[32,16,441]{2,1,0:T(8,128)} copy(f32[32,16,441]{0,1,2:T(8,128)} %bitcast.475) | data formatting | bytes 1806336
  (310 shorter events, 129.6 us)
Async XLA Ops:
  2.1 28.6 %copy-start.44 = (s32[128]{0:T(128)}, s32[128]{0:T(128)S(1)}, u32[]{:S(2)}) copy-start(s32[128]{0:T(128)S(1)} %max.41) | copy-start | bytes 1540
  2.1 28.6 %copy-start.43 = (s32[1024]{0:T(1024)}, s32[1024]{0:T(1024)S(1)}, u32[]{:S(2)}) copy-start(s32[1024]{0:T(1024)S(1)} %pad_clamp_fusion) | copy-start | bytes 12292
  4.1 122.4 %all-to-all-start.2 = ((s32[16,8,128]{2,1,0:T(8,128)}), s32[16,8,128]{2,1,0:T(8,128)}, u32[]{:S(2)}, u32[]{:S(2)}) async-start(s32[16,8,128]{2,1,0:T(8,128)} %bitcast.88), calls=%async_computation.2 | async-start | bytes 131072 | tf_op jit(solution)/shard_map/all_to_all | solution.py:119
  15.9 14.8 %copy-start.1 = (f32[32,16,441]{0,1,2:T(8,128)S(1)}, f32[32,16,441]{0,1,2:T(8,128)}, u32[]{:S(2)}) copy-start(f32[32,16,441]{0,1,2:T(8,128)} %copy.84) | copy-start | bytes 2709508
  32.4 11.7 %copy-start = (s32[32,128]{1,0:T(8,128)S(1)}, s32[32,128]{1,0:T(8,128)}, u32[]{:S(2)}) copy-start(s32[32,128]{1,0:T(8,128)} %param.111) | copy-start | bytes 49156
  47.1 25.0 %copy-start.8 = (f32[32,21,128]{2,1,0:T(8,128)}, f32[32,21,128]{2,1,0:T(8,128)S(1)}, u32[]{:S(2)}) copy-start(f32[32,21,128]{2,1,0:T(8,128)S(1)} %convolution_bitcast_fusion.14) | copy-start | bytes 1032196
  73.4 1.6 copy-start.9
  73.4 1.7 copy-start.40
  76.9 1.6 copy-start.39
  80.4 1.6 copy-start.3
  80.4 1.7 copy-start.38
  82.1 4.4 %copy-start.27 = (f32[27,1,21,21]{0,1,3,2:T(1,128)S(1)}, f32[27,1,21,21]{0,1,3,2:T(1,128)}, u32[]{:S(2)}) copy-start(f32[27,1,21,21]{0,1,3,2:T(1,128)} %slice.1990) | copy-start | bytes 142888
  87.4 3.5 %copy-start.34 = (f32[26,1,21,21]{0,1,3,2:T(1,128)S(1)}, f32[26,1,21,21]{0,1,3,2:T(1,128)}, u32[]{:S(2)}) copy-start(f32[26,1,21,21]{0,1,3,2:T(1,128)} %slice.1995) | copy-start | bytes 137596
  90.9 4.4 %copy-start.33 = (f32[25,1,21,21]{0,1,3,2:T(1,128)S(1)}, f32[25,1,21,21]{0,1,3,2:T(1,128)}, u32[]{:S(2)}) copy-start(f32[25,1,21,21]{0,1,3,2:T(1,128)} %slice.2000) | copy-start | bytes 132304
  95.3 2.5 copy-start.32
  103.1 5.3 %copy-start.2 = (f32[32,16,441]{2,1,0:T(8,128)S(1)}, f32[32,16,441]{2,1,0:T(8,128)}, u32[]{:S(2)}) copy-start(f32[32,16,441]{2,1,0:T(8,128)} %param.113) | copy-start | bytes 2709508
  104.9 54.1 %collective-permute-start = (f32[16,21,128]{2,1,0:T(8,128)}, f32[16,21,128]{2,1,0:T(8,128)}, u32[]{:S(2)}, u32[]{:S(2)}) collective-permute-start(f32[16,21,128]{2,1,0:T(8,128)} %get-tuple-element.668), channel_id=1, source_target_pairs={{0,1},{1,2},{2,3},{3,4},{4,5},{5,6},{6,7},{7,8},{8,9},{9,10},{10,1... | collective-permute-start | bytes 516104 | tf_op jit(solution)/shard_map/ppermute | solution.py:12
  111.4 4.3 %copy-start.41 = (s32[1,16,8]{1,2,0:T(8,128)S(1)}, s32[1,16,8]{1,2,0:T(8,128)}, u32[]{:S(2)}) copy-start(s32[1,16,8]{1,2,0:T(8,128)} %param.115) | copy-start | bytes 1540
  111.4 4.3 %copy-start.42 = (s32[1,16,8]{1,2,0:T(8,128)S(1)}, s32[1,16,8]{1,2,0:T(8,128)}, u32[]{:S(2)}) copy-start(s32[1,16,8]{1,2,0:T(8,128)} %param.116) | copy-start | bytes 1540
  113.4 9.1 %copy-start.26 = (f32[1,16,8,441]{3,2,1,0:T(8,128)S(1)}, f32[1,16,8,441]{3,2,1,0:T(8,128)}, u32[]{:S(2)}) copy-start(f32[1,16,8,441]{3,2,1,0:T(8,128)} %param.114) | copy-start | bytes 677380
  113.4 51.4 %collective-permute-start.1 = (f32[16,16,21,21]{3,1,2,0:T(8,128)}, f32[16,16,21,21]{3,1,2,0:T(8,128)}, u32[]{:S(2)}, u32[]{:S(2)}) collective-permute-start(f32[16,16,21,21]{3,1,2,0:T(8,128)} %copy.117), channel_id=1, source_target_pairs={{0,1},{1,2},{2,3},{3,4},{4,5},{5,6},{6,7},{7,8},{8,9},{9,10},{10,1... | collective-permute-start | bytes 1354760 | tf_op jit(solution)/shard_map/ppermute | solution.py:12
  126.5 25.1 %all-to-all-start = ((f32[16,8,441]{2,1,0:T(8,128)}), f32[16,8,441]{2,1,0:T(8,128)}, u32[]{:S(2)}, u32[]{:S(2)}) async-start(f32[16,8,441]{2,1,0:T(8,128)} %bitcast_multiply_fusion), calls=%async_computation | async-start | bytes 524288 | tf_op jit(solution)/shard_map/all_to_all | solution.py:105
  151.6 11.6 %all-to-all-start.1 = ((s32[16,8,128]{2,1,0:T(8,128)}), s32[16,8,128]{2,1,0:T(8,128)S(1)}, u32[]{:S(2)}, u32[]{:S(2)}) async-start(s32[16,8,128]{2,1,0:T(8,128)} %bitcast.480), calls=%async_computation.1 | async-start | bytes 131072 | tf_op jit(solution)/shard_map/all_to_all | solution.py:112
  164.8 10.3 %copy-start.47 = (f32[16]{0:T(128)S(1)}, f32[16]{0:T(128)}, u32[]{:S(2)}) copy-start(f32[16]{0:T(128)} %get-tuple-element.677) | copy-start | bytes 196
  164.8 10.6 %copy-start.48 = (f32[16]{0:T(128)S(1)}, f32[16]{0:T(128)}, u32[]{:S(2)}) copy-start(f32[16]{0:T(128)} %get-tuple-element.691) | copy-start | bytes 196
  180.6 4.4 %copy-start.45 = (s32[128]{0:T(128)S(1)}, s32[128]{0:T(128)}, u32[]{:S(2)}) copy-start(s32[128]{0:T(128)} %copy-done.44) | copy-start | bytes 1540
  181.5 9.3 %copy-start.46 = (f32[128]{0:T(128)S(1)}, f32[128]{0:T(128)}, u32[]{:S(2)}) copy-start(f32[128]{0:T(128)} %param.117) | copy-start | bytes 1540
  182.5 7.9 %collective-permute-start.2 = (f32[16,21,128]{2,1,0:T(8,128)S(1)}, f32[16,21,128]{2,1,0:T(8,128)S(1)}, u32[]{:S(2)}, u32[]{:S(2)}) collective-permute-start(f32[16,21,128]{2,1,0:T(8,128)S(1)} %fusion.73), channel_id=1, source_target_pairs={{1,0},{2,1},{3,2},{4,3},{5,4},{6,5},{7,6},{8,7},{9,8},{10,9},{11,1... | collective-permute-start | bytes 516104 | tf_op jit(solution)/shard_map/ppermute | solution.py:12
  218.0 27.6 %collective-permute-start.3 = (f32[16,21,128]{2,1,0:T(8,128)}, f32[16,21,128]{2,1,0:T(8,128)S(1)}, u32[]{:S(2)}, u32[]{:S(2)}) collective-permute-start(f32[16,21,128]{2,1,0:T(8,128)} %get-tuple-element.667), channel_id=1, source_target_pairs={{1,0},{2,1},{3,2},{4,3},{5,4},{6,5},{7,6},{8,7},{9,8},{10,9},{11,1... | collective-permute-start | bytes 516104 | tf_op jit(solution)/shard_map/ppermute | solution.py:23
  219.9 13.0 %collective-permute-start.4 = (f32[16,21,128]{2,1,0:T(8,128)}, f32[16,21,128]{2,1,0:T(8,128)S(1)}, u32[]{:S(2)}, u32[]{:S(2)}) collective-permute-start(f32[16,21,128]{2,1,0:T(8,128)} %get-tuple-element.666), channel_id=1, source_target_pairs={{0,1},{1,2},{2,3},{3,4},{4,5},{5,6},{6,7},{7,8},{8,9},{9,10},{10,1... | collective-permute-start | bytes 516104 | tf_op jit(solution)/shard_map/ppermute | solution.py:20
  227.2 38.2 %all-to-all-start.3 = ((f32[16,8,21,128]{3,1,2,0:T(8,128)}), f32[16,8,21,128]{3,1,2,0:T(8,128)}, u32[]{:S(2)}, u32[]{:S(2)}) async-start(f32[16,8,21,128]{3,1,2,0:T(8,128)} %copy.147), calls=%async_computation.3 | async-start | bytes 2752512 | tf_op jit(solution)/shard_map/all_to_all | solution.py:164
  239.8 5.8 %copy-start.23 = (f32[32,21,21]{2,1,0:T(8,128)S(1)}, f32[32,21,21]{2,1,0:T(8,128)}, u32[]{:S(2)}) copy-start(f32[32,21,21]{2,1,0:T(8,128)} %fusion.138) | copy-start | bytes 169348
  240.1 6.8 %copy-start.25 = (f32[32,21,21]{2,1,0:T(8,128)S(1)}, f32[32,21,21]{2,1,0:T(8,128)}, u32[]{:S(2)}) copy-start(f32[32,21,21]{2,1,0:T(8,128)} %fusion.139) | copy-start | bytes 169348
  240.1 8.0 %copy-start.24 = (f32[32,21,21]{2,1,0:T(8,128)S(1)}, f32[32,21,21]{2,1,0:T(8,128)}, u32[]{:S(2)}) copy-start(f32[32,21,21]{2,1,0:T(8,128)} %fusion.140) | copy-start | bytes 169348
  243.3 6.1 %copy-start.22 = (f32[32,21,21]{2,1,0:T(8,128)S(1)}, f32[32,21,21]{2,1,0:T(8,128)}, u32[]{:S(2)}) copy-start(f32[32,21,21]{2,1,0:T(8,128)} %fusion.141) | copy-start | bytes 169348
  243.3 7.3 %copy-start.21 = (f32[32,21,21]{2,1,0:T(8,128)S(1)}, f32[32,21,21]{2,1,0:T(8,128)}, u32[]{:S(2)}) copy-start(f32[32,21,21]{2,1,0:T(8,128)} %fusion.142) | copy-start | bytes 169348
  243.3 8.6 %copy-start.20 = (f32[32,21,21]{2,1,0:T(8,128)S(1)}, f32[32,21,21]{2,1,0:T(8,128)}, u32[]{:S(2)}) copy-start(f32[32,21,21]{2,1,0:T(8,128)} %fusion.143) | copy-start | bytes 169348
  243.3 53.8 %collective-permute-start.5 = (f32[16,16,21,21]{3,1,2,0:T(8,128)}, f32[16,16,21,21]{3,1,2,0:T(8,128)}, u32[]{:S(2)}, u32[]{:S(2)}) collective-permute-start(f32[16,16,21,21]{3,1,2,0:T(8,128)} %copy.144), channel_id=1, source_target_pairs={{1,0},{2,1},{3,2},{4,3},{5,4},{6,5},{7,6},{8,7},{9,8},{10,9},{11,1... | collective-permute-start | bytes 1354760 | tf_op jit(solution)/shard_map/ppermute | solution.py:12
  246.9 6.2 %copy-start.19 = (f32[32,21,21]{2,1,0:T(8,128)S(1)}, f32[32,21,21]{2,1,0:T(8,128)}, u32[]{:S(2)}) copy-start(f32[32,21,21]{2,1,0:T(8,128)} %fusion.144) | copy-start | bytes 169348
  248.1 6.2 %copy-start.18 = (f32[32,21,21]{2,1,0:T(8,128)S(1)}, f32[32,21,21]{2,1,0:T(8,128)}, u32[]{:S(2)}) copy-start(f32[32,21,21]{2,1,0:T(8,128)} %fusion.145) | copy-start | bytes 169348
  249.4 6.2 %copy-start.17 = (f32[32,21,21]{2,1,0:T(8,128)S(1)}, f32[32,21,21]{2,1,0:T(8,128)}, u32[]{:S(2)}) copy-start(f32[32,21,21]{2,1,0:T(8,128)} %fusion.146) | copy-start | bytes 169348
  250.6 6.2 %copy-start.16 = (f32[32,21,21]{2,1,0:T(8,128)S(1)}, f32[32,21,21]{2,1,0:T(8,128)}, u32[]{:S(2)}) copy-start(f32[32,21,21]{2,1,0:T(8,128)} %fusion.147) | copy-start | bytes 169348
  251.8 6.2 %copy-start.15 = (f32[32,21,21]{2,1,0:T(8,128)S(1)}, f32[32,21,21]{2,1,0:T(8,128)}, u32[]{:S(2)}) copy-start(f32[32,21,21]{2,1,0:T(8,128)} %fusion.148) | copy-start | bytes 169348
  253.1 6.2 %copy-start.14 = (f32[32,21,21]{2,1,0:T(8,128)S(1)}, f32[32,21,21]{2,1,0:T(8,128)}, u32[]{:S(2)}) copy-start(f32[32,21,21]{2,1,0:T(8,128)} %fusion.149) | copy-start | bytes 169348
  254.3 6.2 %copy-start.13 = (f32[32,21,21]{2,1,0:T(8,128)S(1)}, f32[32,21,21]{2,1,0:T(8,128)}, u32[]{:S(2)}) copy-start(f32[32,21,21]{2,1,0:T(8,128)} %fusion.150) | copy-start | bytes 169348
  255.5 6.2 %copy-start.12 = (f32[32,21,21]{2,1,0:T(8,128)S(1)}, f32[32,21,21]{2,1,0:T(8,128)}, u32[]{:S(2)}) copy-start(f32[32,21,21]{2,1,0:T(8,128)} %fusion.151) | copy-start | bytes 169348
  256.8 6.2 %copy-start.11 = (f32[32,21,21]{2,1,0:T(8,128)S(1)}, f32[32,21,21]{2,1,0:T(8,128)}, u32[]{:S(2)}) copy-start(f32[32,21,21]{2,1,0:T(8,128)} %fusion.152) | copy-start | bytes 169348
  273.6 39.9 %all-to-all-start.4 = ((f32[16,8,441]{2,1,0:T(8,128)}), f32[16,8,441]{2,1,0:T(8,128)S(1)}, u32[]{:S(2)}, u32[]{:S(2)}) async-start(f32[16,8,441]{2,1,0:T(8,128)} %reshape.1685), calls=%async_computation.4 | async-start | bytes 524288 | tf_op jit(solution)/shard_map/all_to_all | solution.py:168
  (12 other events, 13.0 us)
where the time goes:
time: 319 us; the launch traced here: 315 us
  local copies, waits for them, and re-layouts  105 us (33%)
  matrix products  98.6 us (31%)
  starting transfers between devices  48.7 us (15%)
  waiting for transfers between devices  37.6 us (12%)
  other arithmetic  22.7 us (7%)
    unnamed x134, local copies, waits for them, and re-layouts  29.5 us
    dot_general x17, matrix products, pair_terms(): first = jnp.einsum('san,sbn->sab', left_res, right_hot, precision=precise)  25.1 us
    dot_general x33, matrix products, pull_columns(): return jnp.einsum('sab,sbn->san', blocks, one_hot, precision=precise)  24.2 us
    dot_general x17, matrix products, pair_terms(): jnp.einsum('san,sbn->sab', left_hot, right_res, precision=precise)  22.4 us
    ppermute x4, waiting for transfers between devices, shifted(): return lax.ppermute(value, axis, pairs)  20.5 us
    dot_general x17, matrix products, lift_rows(): return jnp.einsum('sab,san->sbn', blocks, one_hot, precision=precise)  17.8 us
    all_to_all x1, waiting for transfers between devices, on_device(): lax.all_to_all(slot_blocks.reshape(devices, slot_depth, states * states),...  15.5 us
    slice x16, local copies, waits for them, and re-layouts, on_device(): pulled = pull_columns(blocks_now[:kept_rows], one_hot[offset:])  14.8 us
  transfers between devices with their start and end apart: 11, of which 4 were waited for; matrix products, arithmetic and copies ran while one was open for 56% of the time, Pallas kernels for 0%

commit v1 on v0

v1 whole, which is shorter than its diff:
```python
import functools

import jax
import jax.numpy as jnp
import numpy as np
from jax import lax
from jax.experimental import pallas as pl
from jax.experimental.pallas import tpu as pltpu
from jax.sharding import PartitionSpec as P

LANES = 128
SUB = 8
PAD = 32
PER = LANES // PAD
f32, bf16, i32 = jnp.float32, jnp.bfloat16, jnp.int32


def split(x):
    hi = x.astype(bf16)
    return hi, (x - hi.astype(f32)).astype(bf16)


def dot(a, b):
    return jnp.dot(a, b, preferred_element_type=f32)


def dot_nt(a, b):
    return lax.dot_general(a, b, (((1,), (1,)), ((), ())), preferred_element_type=f32)


def lookup(table, index):
    return jnp.take_along_axis(table, index, axis=1, mode="promise_in_bounds")


def iota(shape, dim):
    return lax.broadcasted_iota(i32, shape, dim)


def flip_matrix(states, flat):
    per = LANES // states
    out = np.zeros((flat, -(-states // per) * LANES), np.float32)
    for b in range(states):
        for a in range(states):
            out[a * states + b, (b // per) * LANES + (b % per) * states + a] = 1.0
    return out


def kernel(
    n, depth, band,
    seq_ref, fields_ref, band_ref, contact_ref, start_ref, end_ref, weight_ref, flip_ref,
    gband_ref, gcontact_ref, gfield_ref,
    k4, t4, seql, seqh, seqx, send, recv, cont, ct4, logit, spill_out, spill_in, res, res_in,
    xhi, xlo, rj, rs, rej, dband, dcon, g4, gsend, grecv, gown,
    m_send, m_recv, g_send, g_recv, h_send, h_recv,
):
    rows, seqs = seq_ref.shape
    states = fields_ref.shape[1]
    square = states * states
    nv = k4.shape[0]
    flat = nv * LANES
    nt = t4.shape[0]
    per = LANES // states
    slots = n * depth
    tiles = slots // SUB
    me = lax.axis_index("pos")
    nxt, prv = lax.rem(me + 1, n), lax.rem(me + n - 1, n)

    def peer(k):
        return lax.rem(me + k, n)

    def remote(src, dst, ssem, rsem, to):
        return pltpu.make_async_remote_copy(
            src_ref=src, dst_ref=dst, send_sem=ssem, recv_sem=rsem,
            device_id={"pos": to}, device_id_type=pl.DeviceIdType.MESH,
        )

    def message(k):
        return remote(send.at[peer(k)], recv.at[me], m_send.at[k], m_recv.at[k], peer(k))

    def gradient(k):
        return remote(gsend.at[peer(k)], grecv.at[me], g_send.at[k], g_recv.at[k], peer(k))

    def loop(lo, hi, body):
        def step(k, c):
            body(k)
            return c
        lax.fori_loop(lo, hi, step, 0)

    def tile_of(ref, t, lo, hi):
        if depth == SUB:
            return ref[t, :, lo:hi]
        if depth > SUB:
            each = depth // SUB
            return ref[t // each, pl.ds(pl.multiple_of((t % each) * SUB, SUB), SUB), lo:hi]
        return ref[pl.ds(t * (SUB // depth), SUB // depth), :, lo:hi].reshape(SUB, hi - lo)

    def put_tile(ref, t, lo, hi, value):
        if depth == SUB:
            ref[t, :, lo:hi] = value
        elif depth > SUB:
            each = depth // SUB
            ref[t // each, pl.ds(pl.multiple_of((t % each) * SUB, SUB), SUB), lo:hi] = value
        else:
            ref[pl.ds(t * (SUB // depth), SUB // depth), :, lo:hi] = value.reshape(
                SUB // depth, depth, hi - lo
            )

    barrier = pltpu.get_barrier_semaphore()
    loop(1, n, lambda k: pl.semaphore_signal(
        barrier, inc=1, device_id={"pos": peer(k)}, device_id_type=pl.DeviceIdType.MESH))

    seq_f = seq_ref[...].astype(f32)
    seq_b = seq_f.astype(bf16)
    pick_s = (iota((rows, slots), 0) == start_ref[...]).astype(f32)
    pick_e = (iota((rows, slots), 0) == end_ref[...]).astype(f32)
    pick_st = pick_s.T.astype(bf16)
    pick_et = pick_e.T.astype(bf16)
    pick_cat = jnp.concatenate([pick_s, pick_e], axis=1).astype(bf16)
    send[:, :, flat - LANES : flat] = jnp.zeros((n, depth, LANES), f32)
    send[:, :, :square] = contact_ref[...]
    send[:, :, flat : flat + seqs] = dot(pick_st, seq_b).reshape(n, depth, seqs)
    send[:, :, flat + seqs :] = dot(pick_et, seq_b).reshape(n, depth, seqs)
    recv[me] = send[me]

    pl.semaphore_wait(barrier, n - 1)
    halo = remote(seq_ref.at[pl.ds(0, band)], seqh, h_send.at[0], h_recv.at[0], prv)
    halo.start()
    loop(1, n, lambda k: message(k).start())

    last = jnp.where(me == n - 1, 1, 0)
    row = iota((rows * band, LANES), 0)
    reach = row // band + row % band + 1
    exists = reach + last * rows < 2 * rows
    exists = jnp.where(last == 1, jnp.where(reach < rows, 1, 0), 1) == 1
    for v in range(nv):
        width = min(LANES, square - v * LANES)
        if width == LANES:
            k4[v] = jnp.where(exists, band_ref[:, v * LANES : (v + 1) * LANES], 0.0)
        else:
            k4[v] = jnp.zeros((rows * band, LANES), f32)
            k4[v, :, :width] = jnp.where(
                exists[:, :width], band_ref[:, v * LANES : v * LANES + width], 0.0)
    edge = band * band
    t4[:, :edge, :] = jnp.zeros((nt, edge, LANES), f32)
    t4[:, edge + rows * band :, :] = jnp.zeros((nt, edge, LANES), f32)

    def flip(x):
        hi, lo = split(x)
        return dot(hi, flip_ref[...]) + dot(lo, flip_ref[...])

    chunk = LANES

    def flip_band(c):
        at = pl.multiple_of(c * chunk, chunk)
        out = flip(jnp.concatenate([k4[v, pl.ds(at, chunk), :] for v in range(nv)], axis=1))
        for v in range(nt):
            t4[v, pl.ds(edge + at, chunk), :] = out[:, v * LANES : (v + 1) * LANES]
    loop(0, rows * band // chunk, flip_band)

    seql[...] = jnp.zeros(seql.shape, i32)
    seql[pl.ds(band, rows), :] = seq_ref[...]

    def lift(tables, s):
        return [lookup(tables[b // per], s + (b % per) * states) for b in range(states)]

    def pull(tables, s):
        out = []
        for a in range(states):
            at = a * states + s
            v0, v1 = a * states // LANES, (a * states + states - 1) // LANES
            got = lookup(tables[v0], at & (LANES - 1))
            if v1 != v0:
                got = jnp.where(at >= v1 * LANES, lookup(tables[v1], at & (LANES - 1)), got)
            out.append(got)
        return out

    def lift_step(j0):
        def step(w, acc):
            at = (band + j0 - w) * band + w - 1
            tables = [t4[v, pl.ds(at, SUB, stride=band), :] for v in range(nt)]
            new = lift(tables, seql[pl.ds(band + j0 - w, SUB), :])
            return tuple(x + y for x, y in zip(acc, new))
        return step

    def pull_step(i0):
        def step(w, acc):
            at = i0 * band + w - 1
            tables = [k4[v, pl.ds(at, SUB, stride=band), :] for v in range(nv)]
            new = pull(tables, seqx[pl.ds(i0 + w, SUB), :])
            return tuple(x + y for x, y in zip(acc, new))
        return step

    def lift_range(j0):
        return jnp.maximum(1, j0 - rows + 1), jnp.minimum(band, j0 + SUB - 1) + 1

    zero = jnp.zeros((SUB, seqs), f32)

    def spill_tile(t):
        j0 = rows + t * SUB
        lo, hi = lift_range(j0)
        acc = lax.fori_loop(lo, hi, lift_step(j0), (zero,) * states)
        for b in range(states):
            spill_out[b, pl.ds(pl.multiple_of(t * SUB, SUB), SUB), :] = acc[b]
    loop(0, band // SUB, spill_tile)
    spill = remote(spill_out, spill_in, h_send.at[1], h_recv.at[1], nxt)
    spill.start()

    halo.wait_recv()
    seqx[pl.ds(0, rows), :] = seq_ref[...]
    seqx[pl.ds(rows, band), :] = seqh[...]

    def logit_tile(t):
        i0 = pl.multiple_of(t * SUB, SUB)
        f = fields_ref[pl.ds(i0, SUB), :]
        acc = tuple(jnp.broadcast_to(f[:, a : a + 1], (SUB, seqs)) for a in range(states))
        lo, hi = lift_range(i0)
        acc = lax.fori_loop(lo, hi, lift_step(i0), acc)
        acc = lax.fori_loop(1, band + 1, pull_step(i0), acc)
        for a in range(states):
            logit[a, pl.ds(i0, SUB), :] = acc[a]
    loop(0, rows // SUB, logit_tile)

    loop(1, n, lambda k: message(k).wait_recv())
    flipped = flip(recv[:, :, :flat].reshape(slots, flat))
    for v in range(nt):
        ct4[v] = flipped[:, v * LANES : (v + 1) * LANES]

    def contact_tile(t):
        at = pl.multiple_of(t * SUB, SUB)
        s_end = tile_of(recv, t, flat + seqs, flat + 2 * seqs).astype(i32)
        s_start = tile_of(recv, t, flat, flat + seqs).astype(i32)
        tables = [tile_of(send, t, v * LANES, (v + 1) * LANES) for v in range(nv)]
        for a, x in enumerate(pull(tables, s_end)):
            cont[a, pl.ds(at, SUB), :] = x
        tables = [ct4[v, pl.ds(at, SUB), :] for v in range(nt)]
        for b, x in enumerate(lift(tables, s_start)):
            cont[b, pl.ds(slots + at, SUB), :] = x
    loop(0, tiles, contact_tile)

    spill.wait_recv()

    def add_contacts(a):
        hi, lo = split(cont[a])
        logit[a] = logit[a] + dot(pick_cat, hi) + dot(pick_cat, lo)
        logit[a, pl.ds(0, band), :] = logit[a, pl.ds(0, band), :] + spill_in[a]
    loop(0, states, add_contacts)

    def residual_tile(t):
        i0 = pl.multiple_of(t * SUB, SUB)
        e = [jnp.exp(logit[a, pl.ds(i0, SUB), :]) for a in range(states)]
        total = functools.reduce(lambda x, y: x + y, e)
        s = seq_ref[pl.ds(i0, SUB), :]
        w = weight_ref[...]
        lane = iota((SUB, states), 1)
        field = jnp.zeros((SUB, states), f32)
        for a in range(states):
            r = w * (e[a] / total - (s == a).astype(f32))
            res[a, pl.ds(i0, SUB), :] = r
            field = jnp.where(lane == a, jnp.sum(r, axis=1, keepdims=True), field)
        gfield_ref[pl.ds(i0, SUB), :] = field
    loop(0, rows // SUB, residual_tile)
    back = remote(res.at[:, pl.ds(0, band), :], res_in, h_send.at[2], h_recv.at[2], prv)
    back.start()

    lane = iota((SUB, LANES), 1)
    local = iota((SUB, LANES), 0)
    column = []
    for v in range(nv):
        col = lane + v * LANES
        for a in range(states - 1, 0, -1):
            if a * states <= v * LANES:
                col = lane + (v * LANES - a * states)
                first = a
                break
        else:
            first = 0
        for a in range(first + 1, states):
            if a * states < (v + 1) * LANES:
                col = jnp.where(lane + v * LANES >= a * states, lane + (v * LANES - a * states), col)
        column.append(col & (PAD - 1))

    def assemble(source, w):
        off = local + (w - 1)
        first = (w - 1) // PER
        steps = (w - 1 + SUB - 1) // PER - first
        chosen = {}

        def chosen_rows(a):
            if a not in chosen:
                x = source(a, first)
                for k in range(1, steps + 1):
                    x = jnp.where(off >= (first + k) * PER, source(a, first + k), x)
                chosen[a] = x
            return chosen[a]

        outs = []
        for v in range(nv):
            index = (off & (PER - 1)) * PAD + column[v]
            out = None
            for a in range(states):
                if a * states >= (v + 1) * LANES or (a + 1) * states <= v * LANES:
                    continue
                got = lookup(chosen_rows(a), index)
                out = got if out is None else jnp.where(lane + v * LANES >= a * states, got, out)
            outs.append(out)
        return outs

    for a in range(states):
        hi, lo = split(res[a])
        both = jnp.concatenate([hi, lo], axis=1)
        x = dot(pick_st, both)
        rs[a] = x[:, :seqs] + x[:, seqs:]
        x = dot(pick_et, both)
        rej[pl.ds(a, slots, stride=PAD), :] = x[:, :seqs] + x[:, seqs:]

    def hot_rows(s):
        return jnp.concatenate([(s == a).astype(f32) for a in range(states)], axis=0).astype(bf16)

    def hot_columns(s):
        level = iota((PAD, seqs), 0)
        return jnp.concatenate(
            [(s[r : r + 1] == level).astype(f32) for r in range(s.shape[0])], axis=0).astype(bf16)

    def from_dcon(a, v):
        return dcon[pl.ds(a * SUB, SUB), v * LANES : (v + 1) * LANES]

    def far_half(t):
        s_start = tile_of(recv, t, flat, flat + seqs).astype(i32)
        left = hot_rows(s_start)
        hi, lo = split(rej[pl.ds(pl.multiple_of(t * SUB * PAD, SUB * PAD), SUB * PAD), :])
        dcon[...] = dot_nt(left, hi) + dot_nt(left, lo)
        for v, x in enumerate(assemble(from_dcon, 1)):
            put_tile(gsend, t, v * LANES, (v + 1) * LANES, x)

    if depth == SUB:
        def far_step(k):
            far_half(peer(k))
            gradient(k).start()
        loop(1, n, far_step)
        far_half(me)
    else:
        loop(0, tiles, far_half)
        loop(1, n, lambda k: gradient(k).start())
    grecv[me] = gsend[me]

    def near_half(t):
        s_end = tile_of(recv, t, flat + seqs, flat + 2 * seqs).astype(i32)
        right = hot_columns(s_end)
        at = pl.multiple_of(t * SUB, SUB)
        hi, lo = split(rs[:, pl.ds(at, SUB), :].reshape(states * SUB, seqs))
        dcon[...] = dot_nt(hi, right) + dot_nt(lo, right)
        for v, x in enumerate(assemble(from_dcon, 1)):
            put_tile(gown, t, v * LANES, (v + 1) * LANES, x)
    loop(0, tiles, near_half)

    for a in range(states):
        rj[pl.ds(a, rows, stride=PAD), :] = res[a]
    back.wait_recv()
    for a in range(states):
        rj[pl.ds(rows * PAD + a, band, stride=PAD), :] = res_in[a]

    def columns_of(t):
        h = hot_columns(seqx[pl.ds(pl.multiple_of(t * SUB, SUB), SUB), :])
        at = pl.multiple_of(t * SUB * PAD, SUB * PAD)
        hi, lo = split(rj[pl.ds(at, SUB * PAD), :])
        xhi[pl.ds(at, SUB * PAD), :] = jnp.concatenate([h, hi], axis=1)
        xlo[pl.ds(at, SUB * PAD), :] = jnp.concatenate([h, lo], axis=1)
    loop(0, (rows + band) // SUB, columns_of)
    reached = dband.shape[1]

    def from_dband(a, v):
        return dband[pl.ds(a * SUB, SUB), v * LANES : (v + 1) * LANES]

    def band_tile(t):
        i0 = pl.multiple_of(t * SUB, SUB)
        hi, lo = split(res[:, pl.ds(i0, SUB), :].reshape(states * SUB, seqs))
        h = hot_rows(seq_ref[pl.ds(i0, SUB), :])
        at = pl.ds(pl.multiple_of((i0 + 1) * PAD, PAD), reached)
        dband[...] = dot_nt(jnp.concatenate([hi, h], axis=1), xhi[at, :]) + dot_nt(
            jnp.concatenate([lo, h], axis=1), xlo[at, :])
        for w in range(1, band + 1):
            for v, x in enumerate(assemble(from_dband, w)):
                g4[v, pl.ds(i0 * band + w - 1, SUB, stride=band), :] = x
    loop(0, rows // SUB, band_tile)

    for v in range(nv):
        width = min(LANES, square - v * LANES)
        gband_ref[:, v * LANES : v * LANES + width] = jnp.where(
            exists[:, :width], g4[v, :, :width], 0.0)

    loop(1, n, lambda k: gradient(k).wait_recv())
    gcontact_ref[...] = gown[:, :, :square] + grecv[:, :, :square]

    halo.wait_send()
    spill.wait_send()
    back.wait_send()

    def drain(k):
        message(k).wait_send()
        gradient(k).wait_send()
    loop(1, n, drain)


def on_device(sequences, fields, band_coupling, contact_coupling, slot_start, slot_end, seq_weight):
    rows, seqs = sequences.shape
    states = fields.shape[1]
    band = band_coupling.shape[1]
    n, depth = contact_coupling.shape[1:3]
    square = states * states
    slots = n * depth
    nv = -(-square // LANES)
    flat = nv * LANES
    flip = flip_matrix(states, flat)
    nt = flip.shape[1] // LANES
    near = SUB + band - 1
    reached = -(-near // SUB) * SUB * PAD
    columns = (rows - SUB + 1) * PAD + reached
    V = pltpu.VMEM
    scratch = [
        V((nv, rows * band, LANES), f32),
        V((nt, (rows + 2 * band) * band, LANES), f32),
        V((rows + 2 * band, seqs), i32),
        V((band, seqs), i32),
        V((rows + band, seqs), i32),
        V((n, depth, flat + 2 * seqs), f32),
        V((n, depth, flat + 2 * seqs), f32),
        V((states, 2 * slots, seqs), f32),
        V((nt, slots, LANES), f32),
        V((states, rows, seqs), f32),
        V((states, band, seqs), f32),
        V((states, band, seqs), f32),
        V((states, rows, seqs), f32),
        V((states, band, seqs), f32),
        V((columns, 2 * seqs), bf16),
        V((columns, 2 * seqs), bf16),
        V(((rows + band) * PAD, seqs), f32),
        V((states, slots, seqs), f32),
        V((slots * PAD, seqs), f32),
        V((states * SUB, reached), f32),
        V((states * SUB, SUB * PAD), f32),
        V((nv, rows * band, LANES), f32),
        V((n, depth, flat), f32),
        V((n, depth, flat), f32),
        V((n, depth, flat), f32),
        pltpu.SemaphoreType.DMA((n,)),
        pltpu.SemaphoreType.DMA((n,)),
        pltpu.SemaphoreType.DMA((n,)),
        pltpu.SemaphoreType.DMA((n,)),
        pltpu.SemaphoreType.DMA((3,)),
        pltpu.SemaphoreType.DMA((3,)),
    ]
    gband, gcontact, gfield = pl.pallas_call(
        functools.partial(kernel, n, depth, band),
        out_shape=(
            jax.ShapeDtypeStruct((rows * band, square), f32),
            jax.ShapeDtypeStruct((n, depth, square), f32),
            jax.ShapeDtypeStruct((rows, states), f32),
        ),
        in_specs=[pl.BlockSpec(memory_space=V)] * 8,
        out_specs=(pl.BlockSpec(memory_space=V),) * 3,
        scratch_shapes=scratch,
        compiler_params=pltpu.CompilerParams(
            collective_id=0, has_side_effects=True, vmem_limit_bytes=50 * 2**20),
    )(
        sequences,
        fields,
        band_coupling.reshape(rows * band, square),
        contact_coupling[0],
        slot_start.reshape(1, slots),
        slot_end.reshape(1, slots),
        seq_weight.reshape(1, seqs),
        jnp.asarray(flip, bf16),
    )
    return gband.reshape(rows, band, square), gcontact[None], gfield


def solution(mesh):
    in_specs = (
        P(("grp", "pos"), None),
        P(("grp", "pos"), None),
        P(("grp", "pos"), None, None),
        P(("grp", "pos"), None, None, None),
        P(("grp", "pos"), None, None),
        P(("grp", "pos"), None, None),
        P("grp"),
    )
    out_specs = (
        P(("grp", "pos"), None, None),
        P(("grp", "pos"), None, None, None),
        P(("grp", "pos"), None),
    )
    return jax.shard_map(
        on_device, mesh=mesh, in_specs=in_specs, out_specs=out_specs, check_vma=False
    )
```

time: 319 us -> 60.5 us (0.19)
  the two profiles are of different devices: /device:TPU:11 before, /device:TPU:0 now
where the time goes in v1:
time: 60.5 us; the launch traced here: 60.1 us
  Pallas kernels  51 us (84%)
  local copies, waits for them, and re-layouts  8.42 us (14%)
  between operations  0.66 us (1%)
    pallas_call x1, Pallas kernels, on_device(): pl.pallas_call(functools.partial(kernel, n, depth, band), out_shape=(jax....  51 us
    unnamed x22, local copies, waits for them, and re-layouts  8.25 us

profile of v1, /device:TPU:0, one launch (start us, length us, event | category | flops | bytes accessed | tf_op | source)
XLA Modules:
  0.0 60.1 jit_solution(3967228787953731405)
XLA Ops:
  0.6 0.0 copy-start.6
  0.6 0.7 %copy-done.6 = s32[1,16,8]{1,2,0:T(8,128)S(1)} copy-done((s32[1,16,8]{1,2,0:T(8,128)S(1)}, s32[1,16,8]{1,2,0:T(8,128)}, u32[]{:S(2)}) %copy-start.6) | copy-done | bytes 536
  1.3 0.1 copy.15
  1.4 0.0 copy-start.7
  1.4 0.1 reshape.22.start_ref
  1.5 0.6 copy-done.7
  2.1 0.0 copy-start.5
  2.1 0.1 copy.16
  2.2 0.1 reshape.23.end_ref
  2.2 0.5 copy-done.5
  2.8 0.0 copy-start.3
  2.8 0.0 copy-start.4
  2.8 0.1 copy.17.fields_ref
  2.9 0.6 %copy-done.3 = s32[32,128]{1,0:T(8,128)S(1)} copy-done((s32[32,128]{1,0:T(8,128)S(1)}, s32[32,128]{1,0:T(8,128)}, u32[]{:S(2)}) %copy-start.3) | copy-done | bytes 16408
  3.5 0.0 copy-done.4
  3.5 0.0 copy-start
  3.5 1.2 %copy-done = f32[32,16,441]{2,1,0:T(8,128)S(1)} copy-done((f32[32,16,441]{2,1,0:T(8,128)S(1)}, f32[32,16,441]{2,1,0:T(8,128)}, u32[]{:S(2)}) %copy-start) | copy-done | bytes 903192
  4.7 0.0 copy-start.1
  4.7 1.0 %copy-done.1 = bf16[512,512]{1,0:T(8,128)(2,1)S(1)} copy-done((bf16[512,512]{1,0:T(8,128)(2,1)S(1)}, bf16[512,512]{1,0:T(8,128)(2,1)}, u32[]{:S(2)}) %copy-start.1) | copy-done | bytes 524312
  5.8 0.0 copy-start.2
  5.8 0.9 %copy-done.2 = f32[1,16,8,441]{3,2,1,0:T(8,128)S(1)} copy-done((f32[1,16,8,441]{3,2,1,0:T(8,128)S(1)}, f32[1,16,8,441]{3,2,1,0:T(8,128)}, u32[]{:S(2)}) %copy-start.2) | copy-done | bytes 225816
  6.7 51.0 %shard_map.103 = (f32[512,441]{1,0:T(8,128)S(1)}, f32[16,8,441]{2,1,0:T(8,128)S(1)}, f32[32,21]{1,0:T(8,128)S(1)}) custom-call(s32[32,128]{1,0:T(8,128)S(1)} %copy-done.3, f32[32,21]{1,0:T(8,128)S(1)} %copy.17.fields_ref, f32[512,441]{1,0:T(8,128)S(1)} %bitcast.5, f32[16,8,441]{2,1,0:T(8,128)S(1)} %bitcast.8, s32[1,128]{1,0:T(1,128)S(1)} %reshape.22.start_ref, ...), custom_call_target="tpu_custom_call" | custom-call | tf_op jit(solution)/shard_map/pallas_call | solution.py:452
  57.7 0.7 %copy.18 = f32[32,21]{0,1:T(8,128)} copy(f32[32,21]{1,0:T(8,128)S(1)} %get-tuple-element.14) | data formatting | bytes 5376
  58.4 1.0 %copy.21 = f32[32,16,441]{2,1,0:T(8,128)} copy(f32[32,16,441]{2,1,0:T(8,128)S(1)} %bitcast.6) | data formatting | bytes 1806336
  59.4 0.7 %copy.22 = f32[1,16,8,441]{3,2,1,0:T(8,128)} copy(f32[1,16,8,441]{3,2,1,0:T(8,128)S(1)} %bitcast.7) | data formatting | bytes 451584
Async XLA Ops:
  0.6 0.7 %copy-start.6 = (s32[1,16,8]{1,2,0:T(8,128)S(1)}, s32[1,16,8]{1,2,0:T(8,128)}, u32[]{:S(2)}) copy-start(s32[1,16,8]{1,2,0:T(8,128)} %param.12) | copy-start | bytes 1540
  1.4 0.7 %copy-start.7 = (s32[1,16,8]{1,2,0:T(8,128)S(1)}, s32[1,16,8]{1,2,0:T(8,128)}, u32[]{:S(2)}) copy-start(s32[1,16,8]{1,2,0:T(8,128)} %param.13) | copy-start | bytes 1540
  2.1 0.7 %copy-start.5 = (f32[32,21]{0,1:T(8,128)S(1)}, f32[32,21]{0,1:T(8,128)}, u32[]{:S(2)}) copy-start(f32[32,21]{0,1:T(8,128)} %param.9) | copy-start | bytes 8068
  2.8 0.7 %copy-start.3 = (s32[32,128]{1,0:T(8,128)S(1)}, s32[32,128]{1,0:T(8,128)}, u32[]{:S(2)}) copy-start(s32[32,128]{1,0:T(8,128)} %seq_ref.1) | copy-start | bytes 49156
  2.8 0.7 %copy-start.4 = (f32[128]{0:T(128)S(1)}, f32[128]{0:T(128)}, u32[]{:S(2)}) copy-start(f32[128]{0:T(128)} %param.14) | copy-start | bytes 1540
  3.5 1.2 %copy-start = (f32[32,16,441]{2,1,0:T(8,128)S(1)}, f32[32,16,441]{2,1,0:T(8,128)}, u32[]{:S(2)}) copy-start(f32[32,16,441]{2,1,0:T(8,128)} %param.10) | copy-start | bytes 2709508
  4.7 1.0 %copy-start.1 = (bf16[512,512]{1,0:T(8,128)(2,1)S(1)}, bf16[512,512]{1,0:T(8,128)(2,1)}, u32[]{:S(2)}) copy-start(bf16[512,512]{1,0:T(8,128)(2,1)} %constant.2.clone.flip_ref) | copy-start | bytes 1572868
  5.8 0.9 %copy-start.2 = (f32[1,16,8,441]{3,2,1,0:T(8,128)S(1)}, f32[1,16,8,441]{3,2,1,0:T(8,128)}, u32[]{:S(2)}) copy-start(f32[1,16,8,441]{3,2,1,0:T(8,128)} %param.11) | copy-start | bytes 677380

commit v2 on v1

--- a/solution.py
+++ b/solution.py
@@ -47,12 +47,23 @@
 
 def kernel(
     n, depth, band,
-    seq_ref, fields_ref, band_ref, contact_ref, start_ref, end_ref, weight_ref, flip_ref,
+    seq_hbm, start_hbm, end_hbm, contact_hbm, band_hbm, flip_hbm, fields_hbm, weight_hbm,
     gband_ref, gcontact_ref, gfield_ref,
     k4, t4, seql, seqh, seqx, send, recv, cont, ct4, logit, spill_out, spill_in, res, res_in,
-    xhi, xlo, rj, rs, rej, dband, dcon, g4, gsend, grecv, gown,
+    xhi, xlo, rj, rs, rej, dband, g4, gsend, grecv, gown,
     m_send, m_recv, g_send, g_recv, h_send, h_recv,
+    seq_ref, start_ref, end_ref, contact_ref, band_ref, flip_ref, fields_ref, weight_ref, in_sem,
 ):
+    loads = [
+        pltpu.make_async_copy(src, dst, in_sem.at[i])
+        for i, (src, dst) in enumerate((
+            (seq_hbm, seq_ref), (start_hbm, start_ref), (end_hbm, end_ref),
+            (contact_hbm, contact_ref), (band_hbm, band_ref), (flip_hbm, flip_ref),
+            (fields_hbm, fields_ref), (weight_hbm, weight_ref),
+        ))
+    ]
+    for load in loads:
+        load.start()
     rows, seqs = seq_ref.shape
     states = fields_ref.shape[1]
     square = states * states
@@ -80,11 +91,21 @@
     def gradient(k):
         return remote(gsend.at[peer(k)], grecv.at[me], g_send.at[k], g_recv.at[k], peer(k))
 
-    def loop(lo, hi, body):
+    def loop(lo, hi, body, group=1, after=None):
+        while (hi - lo) % group:
+            group -= 1
+
         def step(k, c):
-            body(k)
+            for j in range(group):
+                body(lo + k * group + j)
+            if after is not None:
+                for j in range(group):
+                    after(lo + k * group + j)
             return c
-        lax.fori_loop(lo, hi, step, 0)
+        if hi - lo == group:
+            step(0, 0)
+        else:
+            lax.fori_loop(0, (hi - lo) // group, step, 0)
 
     def tile_of(ref, t, lo, hi):
         if depth == SUB:
@@ -108,6 +129,9 @@
     barrier = pltpu.get_barrier_semaphore()
     loop(1, n, lambda k: pl.semaphore_signal(
         barrier, inc=1, device_id={"pos": peer(k)}, device_id_type=pl.DeviceIdType.MESH))
+
+    for load in loads[:4]:
+        load.wait()
 
     seq_f = seq_ref[...].astype(f32)
     seq_b = seq_f.astype(bf16)
@@ -126,6 +150,9 @@
     halo = remote(seq_ref.at[pl.ds(0, band)], seqh, h_send.at[0], h_recv.at[0], prv)
     halo.start()
     loop(1, n, lambda k: message(k).start())
+
+    for load in loads[4:]:
+        load.wait()
 
     last = jnp.where(me == n - 1, 1, 0)
     row = iota((rows * band, LANES), 0)
@@ -155,7 +182,7 @@
         out = flip(jnp.concatenate([k4[v, pl.ds(at, chunk), :] for v in range(nv)], axis=1))
         for v in range(nt):
             t4[v, pl.ds(edge + at, chunk), :] = out[:, v * LANES : (v + 1) * LANES]
-    loop(0, rows * band // chunk, flip_band)
+    loop(0, rows * band // chunk, flip_band, 2)
 
     seql[...] = jnp.zeros(seql.shape, i32)
     seql[pl.ds(band, rows), :] = seq_ref[...]
@@ -191,17 +218,19 @@
         return step
 
     def lift_range(j0):
-        return jnp.maximum(1, j0 - rows + 1), jnp.minimum(band, j0 + SUB - 1) + 1
+        return range(max(1, j0 - rows + 1), min(band, j0 + SUB - 1) + 1)
 
     zero = jnp.zeros((SUB, seqs), f32)
 
     def spill_tile(t):
         j0 = rows + t * SUB
-        lo, hi = lift_range(j0)
-        acc = lax.fori_loop(lo, hi, lift_step(j0), (zero,) * states)
+        acc = (zero,) * states
+        for w in lift_range(j0):
+            acc = lift_step(j0)(w, acc)
         for b in range(states):
-            spill_out[b, pl.ds(pl.multiple_of(t * SUB, SUB), SUB), :] = acc[b]
-    loop(0, band // SUB, spill_tile)
+            spill_out[b, pl.ds(t * SUB, SUB), :] = acc[b]
+    for t in range(band // SUB):
+        spill_tile(t)
     spill = remote(spill_out, spill_in, h_send.at[1], h_recv.at[1], nxt)
     spill.start()
 
@@ -210,15 +239,17 @@
     seqx[pl.ds(rows, band), :] = seqh[...]
 
     def logit_tile(t):
-        i0 = pl.multiple_of(t * SUB, SUB)
+        i0 = t * SUB
         f = fields_ref[pl.ds(i0, SUB), :]
         acc = tuple(jnp.broadcast_to(f[:, a : a + 1], (SUB, seqs)) for a in range(states))
-        lo, hi = lift_range(i0)
-        acc = lax.fori_loop(lo, hi, lift_step(i0), acc)
-        acc = lax.fori_loop(1, band + 1, pull_step(i0), acc)
+        for w in lift_range(i0):
+            acc = lift_step(i0)(w, acc)
+        for w in range(1, band + 1):
+            acc = pull_step(i0)(w, acc)
         for a in range(states):
             logit[a, pl.ds(i0, SUB), :] = acc[a]
-    loop(0, rows // SUB, logit_tile)
+    for t in range(rows // SUB):
+        logit_tile(t)
 
     loop(1, n, lambda k: message(k).wait_recv())
     flipped = flip(recv[:, :, :flat].reshape(slots, flat))
@@ -235,7 +266,7 @@
         tables = [ct4[v, pl.ds(at, SUB), :] for v in range(nt)]
         for b, x in enumerate(lift(tables, s_start)):
             cont[b, pl.ds(slots + at, SUB), :] = x
-    loop(0, tiles, contact_tile)
+    loop(0, tiles, contact_tile, 4)
 
     spill.wait_recv()
 
@@ -243,7 +274,7 @@
         hi, lo = split(cont[a])
         logit[a] = logit[a] + dot(pick_cat, hi) + dot(pick_cat, lo)
         logit[a, pl.ds(0, band), :] = logit[a, pl.ds(0, band), :] + spill_in[a]
-    loop(0, states, add_contacts)
+    loop(0, states, add_contacts, 7)
 
     def residual_tile(t):
         i0 = pl.multiple_of(t * SUB, SUB)
@@ -258,7 +289,7 @@
             res[a, pl.ds(i0, SUB), :] = r
             field = jnp.where(lane == a, jnp.sum(r, axis=1, keepdims=True), field)
         gfield_ref[pl.ds(i0, SUB), :] = field
-    loop(0, rows // SUB, residual_tile)
+    loop(0, rows // SUB, residual_tile, 4)
     back = remote(res.at[:, pl.ds(0, band), :], res_in, h_send.at[2], h_recv.at[2], prv)
     back.start()
 
@@ -321,25 +352,22 @@
         return jnp.concatenate(
             [(s[r : r + 1] == level).astype(f32) for r in range(s.shape[0])], axis=0).astype(bf16)
 
-    def from_dcon(a, v):
-        return dcon[pl.ds(a * SUB, SUB), v * LANES : (v + 1) * LANES]
+    def pick_from(d):
+        return lambda a, v: d[a * SUB : (a + 1) * SUB, v * LANES : (v + 1) * LANES]
 
     def far_half(t):
         s_start = tile_of(recv, t, flat, flat + seqs).astype(i32)
         left = hot_rows(s_start)
         hi, lo = split(rej[pl.ds(pl.multiple_of(t * SUB * PAD, SUB * PAD), SUB * PAD), :])
-        dcon[...] = dot_nt(left, hi) + dot_nt(left, lo)
-        for v, x in enumerate(assemble(from_dcon, 1)):
+        d = dot_nt(left, hi) + dot_nt(left, lo)
+        for v, x in enumerate(assemble(pick_from(d), 1)):
             put_tile(gsend, t, v * LANES, (v + 1) * LANES, x)
 
     if depth == SUB:
-        def far_step(k):
-            far_half(peer(k))
-            gradient(k).start()
-        loop(1, n, far_step)
+        loop(1, n, lambda k: far_half(peer(k)), 5, lambda k: gradient(k).start())
         far_half(me)
     else:
-        loop(0, tiles, far_half)
+        loop(0, tiles, far_half, 4)
         loop(1, n, lambda k: gradient(k).start())
     grecv[me] = gsend[me]
 
@@ -348,10 +376,10 @@
         right = hot_columns(s_end)
         at = pl.multiple_of(t * SUB, SUB)
         hi, lo = split(rs[:, pl.ds(at, SUB), :].reshape(states * SUB, seqs))
-        dcon[...] = dot_nt(hi, right) + dot_nt(lo, right)
-        for v, x in enumerate(assemble(from_dcon, 1)):
+        d = dot_nt(hi, right) + dot_nt(lo, right)
+        for v, x in enumerate(assemble(pick_from(d), 1)):
             put_tile(gown, t, v * LANES, (v + 1) * LANES, x)
-    loop(0, tiles, near_half)
+    loop(0, tiles, near_half, 4)
 
     for a in range(states):
         rj[pl.ds(a, rows, stride=PAD), :] = res[a]
@@ -365,23 +393,29 @@
         hi, lo = split(rj[pl.ds(at, SUB * PAD), :])
         xhi[pl.ds(at, SUB * PAD), :] = jnp.concatenate([h, hi], axis=1)
         xlo[pl.ds(at, SUB * PAD), :] = jnp.concatenate([h, lo], axis=1)
-    loop(0, (rows + band) // SUB, columns_of)
-    reached = dband.shape[1]
-
-    def from_dband(a, v):
-        return dband[pl.ds(a * SUB, SUB), v * LANES : (v + 1) * LANES]
-
-    def band_tile(t):
-        i0 = pl.multiple_of(t * SUB, SUB)
+    loop(0, (rows + band) // SUB, columns_of, 2)
+    reached = dband.shape[2]
+
+    def band_product(t):
+        i0 = t * SUB
         hi, lo = split(res[:, pl.ds(i0, SUB), :].reshape(states * SUB, seqs))
         h = hot_rows(seq_ref[pl.ds(i0, SUB), :])
-        at = pl.ds(pl.multiple_of((i0 + 1) * PAD, PAD), reached)
-        dband[...] = dot_nt(jnp.concatenate([hi, h], axis=1), xhi[at, :]) + dot_nt(
+        at = pl.ds((i0 + 1) * PAD, reached)
+        dband[t % 2] = dot_nt(jnp.concatenate([hi, h], axis=1), xhi[at, :]) + dot_nt(
             jnp.concatenate([lo, h], axis=1), xlo[at, :])
+
+    def band_tile(t):
+        def source(a, v):
+            return dband[t % 2, pl.ds(a * SUB, SUB), v * LANES : (v + 1) * LANES]
         for w in range(1, band + 1):
-            for v, x in enumerate(assemble(from_dband, w)):
-                g4[v, pl.ds(i0 * band + w - 1, SUB, stride=band), :] = x
-    loop(0, rows // SUB, band_tile)
+            for v, x in enumerate(assemble(source, w)):
+                g4[v, pl.ds(t * SUB * band + w - 1, SUB, stride=band), :] = x
+
+    band_product(0)
+    for t in range(rows // SUB):
+        if t + 1 < rows // SUB:
+            band_product(t + 1)
+        band_tile(t)
 
     for v in range(nv):
         width = min(LANES, square - v * LANES)
@@ -436,8 +470,7 @@
         V(((rows + band) * PAD, seqs), f32),
         V((states, slots, seqs), f32),
         V((slots * PAD, seqs), f32),
-        V((states * SUB, reached), f32),
-        V((states * SUB, SUB * PAD), f32),
+        V((2, states * SUB, reached), f32),
         V((nv, rows * band, LANES), f32),
         V((n, depth, flat), f32),
         V((n, depth, flat), f32),
@@ -449,6 +482,18 @@
         pltpu.SemaphoreType.DMA((3,)),
         pltpu.SemaphoreType.DMA((3,)),
     ]
+    operands = (
+        sequences,
+        slot_start.reshape(1, slots),
+        slot_end.reshape(1, slots),
+        contact_coupling[0],
+        band_coupling.reshape(rows * band, square),
+        jnp.asarray(flip, bf16),
+        fields,
+        seq_weight.reshape(1, seqs),
+    )
+    scratch += [V(x.shape, x.dtype) for x in operands]
+    scratch.append(pltpu.SemaphoreType.DMA((len(operands),)))
     gband, gcontact, gfield = pl.pallas_call(
         functools.partial(kernel, n, depth, band),
         out_shape=(
@@ -456,21 +501,12 @@
             jax.ShapeDtypeStruct((n, depth, square), f32),
             jax.ShapeDtypeStruct((rows, states), f32),
         ),
-        in_specs=[pl.BlockSpec(memory_space=V)] * 8,
+        in_specs=[pl.BlockSpec(memory_space=pl.ANY)] * len(operands),
         out_specs=(pl.BlockSpec(memory_space=V),) * 3,
         scratch_shapes=scratch,
         compiler_params=pltpu.CompilerParams(
-            collective_id=0, has_side_effects=True, vmem_limit_bytes=50 * 2**20),
-    )(
-        sequences,
-        fields,
-        band_coupling.reshape(rows * band, square),
-        contact_coupling[0],
-        slot_start.reshape(1, slots),
-        slot_end.reshape(1, slots),
-        seq_weight.reshape(1, seqs),
-        jnp.asarray(flip, bf16),
-    )
+            collective_id=0, has_side_effects=True, vmem_limit_bytes=58 * 2**20),
+    )(*operands)
     return gband.reshape(rows, band, square), gcontact[None], gfield
 
 

time: 60.5 us -> 41.2 us (0.68)
  the two profiles are of different devices: /device:TPU:0 before, /device:TPU:11 now
where the time goes in v2:
time: 41.2 us; the launch traced here: 40.7 us
  Pallas kernels  32.8 us (80%)
  local copies, waits for them, and re-layouts  7.28 us (18%)
  between operations  0.65 us (2%)
    pallas_call x1, Pallas kernels, on_device(): pl.pallas_call(functools.partial(kernel, n, depth, band), out_shape=(jax....  32.8 us
    unnamed x14, local copies, waits for them, and re-layouts  6.07 us

profile of v2, /device:TPU:11, one launch (start us, length us, event | category | flops | bytes accessed | tf_op | source)
XLA Modules:
  0.0 40.7 jit_solution(16936520622231300800)
XLA Ops:
  0.6 0.0 copy-start.2
  0.6 0.7 %copy-done.2 = s32[1,16,8]{1,2,0:T(8,128)S(1)} copy-done((s32[1,16,8]{1,2,0:T(8,128)S(1)}, s32[1,16,8]{1,2,0:T(8,128)}, u32[]{:S(2)}) %copy-start.2) | copy-done | bytes 536
  1.3 0.1 copy.15
  1.4 0.0 copy-start.3
  1.4 0.6 %reshape.21.start_hbm = s32[1,128]{1,0:T(1,128)} reshape(s32[1,16,8]{2,1,0:T(8,128)S(1)} %copy.15) | data formatting | bytes 1024 | tf_op jit(solution)/shard_map/reshape | solution.py:487
  2.0 0.1 copy-done.3
  2.1 0.0 copy-start.1
  2.1 0.1 copy.16
  2.2 0.6 %reshape.22.end_hbm = s32[1,128]{1,0:T(1,128)} reshape(s32[1,16,8]{2,1,0:T(8,128)S(1)} %copy.16) | data formatting | bytes 1024 | tf_op jit(solution)/shard_map/reshape | solution.py:488
  2.8 0.0 copy-done.1
  2.8 0.7 %copy.17.fields_hbm = f32[32,21]{1,0:T(8,128)} copy(f32[32,21]{0,1:T(8,128)S(1)} %copy-done.1) | data formatting | bytes 5376 | tf_op args[1]
  3.5 32.8 %shard_map.103 = (f32[512,441]{1,0:T(8,128)}, f32[16,8,441]{2,1,0:T(8,128)}, f32[32,21]{1,0:T(8,128)}) custom-call(s32[32,128]{1,0:T(8,128)} %seq_hbm.1, s32[1,128]{1,0:T(1,128)} %reshape.21.start_hbm, s32[1,128]{1,0:T(1,128)} %reshape.22.end_hbm, f32[16,8,441]{2,1,0:T(8,128)} %bitcast.8, f32[512,441]{1,0:T(8,128)} %bitcast.5, ...), custom_call_target="tpu_custom_call" | custom-call | tf_op jit(solution)/shard_map/pallas_call | solution.py:497
  36.3 1.4 %copy.18 = f32[32,21]{0,1:T(8,128)} copy(f32[32,21]{1,0:T(8,128)} %get-tuple-element.14) | data formatting | bytes 5376
  37.7 0.0 copy-start
  37.7 2.3 %copy.21 = f32[32,16,441]{2,1,0:T(8,128)} copy(f32[32,16,441]{2,1,0:T(8,128)} %bitcast.6) | data formatting | bytes 1806336
  40.0 0.0 copy-done
  40.0 0.7 %copy.22 = f32[1,16,8,441]{3,2,1,0:T(8,128)} copy(f32[1,16,8,441]{3,2,1,0:T(8,128)S(1)} %bitcast.7) | data formatting | bytes 451584
Async XLA Ops:
  0.6 0.7 %copy-start.2 = (s32[1,16,8]{1,2,0:T(8,128)S(1)}, s32[1,16,8]{1,2,0:T(8,128)}, u32[]{:S(2)}) copy-start(s32[1,16,8]{1,2,0:T(8,128)} %param.12) | copy-start | bytes 1540
  1.4 0.7 %copy-start.3 = (s32[1,16,8]{1,2,0:T(8,128)S(1)}, s32[1,16,8]{1,2,0:T(8,128)}, u32[]{:S(2)}) copy-start(s32[1,16,8]{1,2,0:T(8,128)} %param.13) | copy-start | bytes 1540
  2.1 0.7 %copy-start.1 = (f32[32,21]{0,1:T(8,128)S(1)}, f32[32,21]{0,1:T(8,128)}, u32[]{:S(2)}) copy-start(f32[32,21]{0,1:T(8,128)} %param.9) | copy-start | bytes 8068
  37.7 2.4 %copy-start = (f32[16,8,441]{2,1,0:T(8,128)S(1)}, f32[16,8,441]{2,1,0:T(8,128)}, u32[]{:S(2)}) copy-start(f32[16,8,441]{2,1,0:T(8,128)} %get-tuple-element.7) | copy-start | bytes 677380
